TPU v7x, 32 devices: a whole 2x2x4 slice. The times are simulated.
32 devices in a mesh: shift: 4 (over y, x), sub: 8 (over z, core).
Axes of the slice: x: 2, y: 2, z: 4, core: 2. Of those that a mesh axis runs over, the one named last changes fastest.
Arguments:
- interior_rhs: bfloat16 [8, 1024, 384], P('sub'), may hold values from -6 to 6
- interface_rhs: bfloat16 [2048, 384], replicated, may hold values from -6 to 6
- interior_inverse: bfloat16 [8, 8, 1024, 1024], P('shift', 'sub'), may hold values from -0.1875 to 0.1875
- coupling: bfloat16 [8, 1024, 256], P('sub'), may hold values from -0.1875 to 0.1875
- schur_inverse: bfloat16 [8, 2048, 2048], P('shift', 'sub'), may hold values from -0.125 to 0.125
- weights: float32 [8], P('shift'), may hold values from -1 to 1
- owner_sub: int32 [8], replicated, may hold values from 0 to 7, each once
- index_blocks: int32 [8, 256], replicated, may hold values from 0 to 2047, as said below
Outputs:
- filtered: float32 [1024, 8, 384], P('shift', 'sub')
Inputs may be any that keep to these rules, and one draw needn't show every extreme that they name: `index_blocks`: each row holds 256 distinct interface unknowns; of each aligned block of 2048 // 8 interface unknowns a row holds at most 64, and exactly 64 of some block. `owner_sub`: each position names a different substructure.
All inputs are finite; a program needn't handle non-finite values.
Results may differ from a plain program's by a relative error of at most 0.0053.
Values may be sent and summed in bfloat16 or wider, within the bound.
A program may use at most 64 MiB of HBM per device.

v0:
```python
import jax
import jax.numpy as jnp
from jax import lax
from jax.sharding import PartitionSpec as P


def on_device(
    interior_rhs,
    interface_rhs,
    interior_inverse,
    coupling,
    schur_inverse,
    weights,
    owner_sub,
    index_blocks,
):
    position = lax.axis_index("sub")
    substructure = lax.dynamic_index_in_dim(owner_sub, position, 0, keepdims=False)
    idx = lax.dynamic_index_in_dim(index_blocks, substructure, 0, keepdims=False)
    rhs_local = interior_rhs[0]
    couple_local = coupling[0]
    schur_rows = schur_inverse.shape[1]
    columns = rhs_local.shape[1]
    touched = idx.shape[0]
    own_start = position * schur_rows
    owners = lax.axis_size("sub")
    slot_most = max(2, 2 * touched // owners)
    owner_of = idx // schur_rows
    local_row = idx - owner_of * schur_rows
    entries = lax.iota(jnp.int32, touched)
    same_owner = owner_of[None, :] == owner_of[:, None]
    earlier = entries[None, :] < entries[:, None]
    rank = jnp.sum(jnp.logical_and(same_owner, earlier).astype(jnp.int32), axis=1)
    target = owner_of * slot_most + rank
    slot_ids = lax.iota(jnp.int32, owners * slot_most)
    matches = slot_ids[:, None] == target[None, :]
    slot_select = matches.astype(jnp.bfloat16)
    send_ids = (jnp.sum(jnp.where(matches, local_row[None, :] + 1, 0), axis=1) - 1).reshape(
        owners, slot_most
    )
    own_numbers = lax.iota(jnp.int32, schur_rows)
    accumulated = jnp.zeros(rhs_local.shape, jnp.float32)
    for which in range(interior_inverse.shape[0]):
        inverse = interior_inverse[which, 0]
        schur_local = schur_inverse[which]
        eliminated = jnp.dot(inverse, rhs_local, preferred_element_type=jnp.float32).astype(
            jnp.bfloat16
        )
        coupled = lax.dot_general(
            couple_local, eliminated, (((0,), (0,)), ((), ())), preferred_element_type=jnp.float32
        ).astype(jnp.bfloat16)
        rhs_own = lax.dynamic_slice_in_dim(interface_rhs, own_start, schur_rows, 0)
        send_rows = (
            jnp.dot(slot_select, coupled, preferred_element_type=jnp.float32)
            .astype(jnp.bfloat16)
            .reshape(owners, slot_most, columns)
        )
        got_rows, got_ids = (
            lax.all_to_all(send_rows, "sub", split_axis=0, concat_axis=0, tiled=True),
            lax.all_to_all(send_ids, "sub", split_axis=0, concat_axis=0, tiled=True),
        )
        flat_rows = got_rows.reshape(owners * slot_most, columns)
        flat_ids = got_ids.reshape(owners * slot_most)
        receive_select = (own_numbers[:, None] == flat_ids[None, :]).astype(jnp.bfloat16)
        summed_own = jnp.dot(receive_select, flat_rows, preferred_element_type=jnp.float32)
        reduced_own = (rhs_own.astype(jnp.float32) - summed_own).astype(jnp.bfloat16)
        solved = jnp.dot(
            schur_local,
            lax.all_gather(reduced_own, "sub", axis=0, tiled=True),
            preferred_element_type=jnp.float32,
        )
        interface_sol = solved.astype(jnp.bfloat16)
        piece = lax.all_gather(interface_sol, "sub", axis=0, tiled=True)
        sources = lax.iota(jnp.int32, piece.shape[0])
        selector = (idx[:, None] == sources[None, :]).astype(jnp.bfloat16)
        picked = jnp.dot(selector, piece, preferred_element_type=jnp.float32)
        correction = jnp.dot(
            couple_local, picked.astype(jnp.bfloat16), preferred_element_type=jnp.float32
        ).astype(jnp.bfloat16)
        interior_sol = eliminated.astype(jnp.float32) - jnp.dot(
            inverse, correction, preferred_element_type=jnp.float32
        )
        accumulated = accumulated + weights[which] * interior_sol
    share_rows = accumulated.shape[0] // lax.axis_size("shift")
    whole_sum = lax.psum(accumulated, "shift")
    own_rows = lax.dynamic_slice_in_dim(
        whole_sum, lax.axis_index("shift") * share_rows, share_rows, 0
    )
    return own_rows[:, None, :]


def solution(mesh):
    in_specs = (
        P("sub", None, None),
        P(),
        P("shift", "sub", None, None),
        P("sub", None, None),
        P("shift", "sub", None),
        P("shift"),
        P(),
        P(),
    )
    out_specs = P("shift", "sub", None)
    return jax.shard_map(
        on_device, mesh=mesh, in_specs=in_specs, out_specs=out_specs, check_vma=False
    )
```

profile of v0, /device:TPU:1, one launch (start us, length us, event | category | flops | bytes accessed | tf_op | source)
XLA Modules:
  0.0 233.0 jit_solution(8941956732948698194)
XLA Ops:
  6.5 1.3 dynamic_slice.15
  9.8 0.7 subtract_add_fusion
  11.6 6.4 %all-to-all-start = ((s32[8,1,64]{2,1,0:T(1,128)}), s32[8,1,64]{2,1,0:T(1,128)S(1)}, u32[]{:S(2)}, u32[]{:S(2)}) async-start(s32[8,1,64]{2,1,0:T(1,128)} %sub.34), calls=%async_computation | async-start | bytes 8192 | tf_op jit(solution)/shard_map/all_to_all | solution.py:60
  17.9 2.9 %fusion.22 = bf16[1024,384]{1,0:T(8,128)(2,1)S(1)} fusion(bf16[2,1,1024,1024]{3,2,1,0:T(8,128)(2,1)} %param.10, bf16[1,1024,384]{2,1,0:T(8,128)(2,1)S(1)} %copy-done), kind=kOutput, calls=%fused_computation.23 | convolution fusion | flops 805699584 | bytes 3670016 | tf_op jit(solution)/shard_map/dot_general | solution.py:46
  20.9 1.6 convolution_convert_fusion.2
  22.8 4.8 %all-to-all-start.2 = ((bf16[8,64,384]{2,1,0:T(8,128)(2,1)}), bf16[8,64,384]{2,1,0:T(8,128)(2,1)S(1)}, u32[]{:S(2)}, u32[]{:S(2)}) async-start(bf16[8,64,384]{2,1,0:T(8,128)(2,1)} %bitcast.17), calls=%async_computation.2 | async-start | bytes 786432 | tf_op jit(solution)/shard_map/all_to_all | solution.py:59
  28.9 10.4 %all-to-all-done.2 = bf16[8,64,384]{2,1,0:T(8,128)(2,1)S(1)} async-done(((bf16[8,64,384]{2,1,0:T(8,128)(2,1)}), bf16[8,64,384]{2,1,0:T(8,128)(2,1)S(1)}, u32[]{:S(2)}, u32[]{:S(2)}) %all-to-all-start.2) | async-done | bytes 393248 | tf_op jit(solution)/shard_map/all_to_all | solution.py:59
  39.3 1.9 fusion.28
  41.3 3.7 %fusion.19 = bf16[1024,384]{1,0:T(8,128)(2,1)} fusion(bf16[2,1,1024,1024]{3,2,1,0:T(8,128)(2,1)} %param.10, bf16[1,1024,384]{2,1,0:T(8,128)(2,1)S(1)} %copy-done), kind=kOutput, calls=%fused_computation.22 | convolution fusion | flops 805699584 | bytes 3670016 | tf_op jit(solution)/shard_map/dot_general | solution.py:46
  45.0 2.3 convolution_convert_fusion.3
  47.3 25.0 %all_to_all.17 = bf16[8,64,384]{2,1,0:T(8,128)(2,1)S(1)} all-to-all(bf16[8,64,384]{2,1,0:T(8,128)(2,1)S(1)} %bitcast.80), channel_id=1, replica_groups=mesh['shift'=4,'sub'=8] {'sub'}, dimensions={0} | all-to-all | bytes 786432 | tf_op jit(solution)/shard_map/all_to_all | solution.py:59
  72.3 1.9 fusion.27
  74.6 2.7 %fusion.30 = bf16[256,384]{0,1:T(8,128)(2,1)} fusion(bf16[2048,384]{1,0:T(8,128)(2,1)} %all-gather.9.cloned.1.call-done, bf16[2,256,2048]{2,1,0:T(8,128)(2,1)S(1)} %copy-done.2), kind=kOutput, calls=%fused_computation.37 | convolution fusion | flops 402751488 | bytes 2818048 | tf_op jit(solution)/shard_map/dot_general | solution.py:67
  77.5 22.8 %all-gather.5.cloned.1.call-done = bf16[2048,384]{1,0:T(8,128)(2,1)} async-done(((bf16[256,384]{1,0:T(8,128)(2,1)}), bf16[2048,384]{1,0:T(8,128)(2,1)}) %all-gather.5.cloned.1.call-update) | async-done | bytes 1572880 | tf_op jit(solution)/shard_map/all_gather | solution.py:69
  100.3 2.7 %fusion.29 = bf16[256,384]{0,1:T(8,128)(2,1)} fusion(bf16[2048,384]{1,0:T(8,128)(2,1)} %all-gather.5.cloned.1.call-done, bf16[2,256,2048]{2,1,0:T(8,128)(2,1)S(1)} %copy-done.2), kind=kOutput, calls=%fused_computation.36 | convolution fusion | flops 402751488 | bytes 2818048 | tf_op jit(solution)/shard_map/dot_general | solution.py:67
  103.8 24.9 %all-gather.11.cloned.1.call-done = bf16[2048,384]{0,1:T(8,128)(2,1)} async-done(((bf16[256,384]{0,1:T(8,128)(2,1)}), bf16[2048,384]{0,1:T(8,128)(2,1)}) %all-gather.11.cloned.1.call-update) | async-done | bytes 1572880 | tf_op jit(solution)/shard_map/all_gather | solution.py:73
  128.7 2.2 fusion.26
  130.8 3.1 %fusion = f32[384,1024]{0,1:T(8,128)S(1)} fusion(bf16[2,1,1024,1024]{3,2,1,0:T(8,128)(2,1)} %param.10, bf16[256,384]{1,0:T(8,128)(2,1)S(1)} %fusion.26, bf16[1,1024,256]{2,1,0:T(8,128)(2,1)S(1)} %copy-done.4), kind=kOutput, calls=%fused_computation | convolution fusion | flops 1007026176 | bytes 4390912 | tf_op jit(solution)/shard_map/dot_general | solution.py:80
  133.9 22.5 %all-gather.7.cloned.1.call-done = bf16[2048,384]{0,1:T(8,128)(2,1)} async-done(((bf16[256,384]{0,1:T(8,128)(2,1)}), bf16[2048,384]{0,1:T(8,128)(2,1)}) %all-gather.7.cloned.1.call-update) | async-done | bytes 1572880 | tf_op jit(solution)/shard_map/all_gather | solution.py:73
  156.4 2.2 fusion.25
  158.6 6.1 %fusion.15 = f32[1024,384]{1,0:T(8,128)} fusion(f32[384,1024]{0,1:T(8,128)S(1)} %fusion, bf16[1024,384]{1,0:T(8,128)(2,1)} %copy-done.5, bf16[1024,384]{1,0:T(8,128)(2,1)} %fusion.19, bf16[2,1,1024,1024]{3,2,1,0:T(8,128)(2,1)} %param.10, bf16[256,384]{1,0:T(8,128)(2,1)S(1)} %fusion.25, f32[]{:T(128)} %bitcast.15, f32[]{:T(128)} %bitcast, ...), kind=kOutput, calls=%fused_computation.17 | convolution fusion | flops 1009778688 | bytes 7537664 | tf_op jit(solution)/shard_map/dot_general | solution.py:80
  164.7 59.8 %all-reduce.2.cloned.1.call-done = f32[1024,384]{1,0:T(8,128)} async-done(((f32[1024,384]{1,0:T(8,128)}), f32[1024,384]{1,0:T(8,128)}) %all-reduce.2.cloned.1.call-update) | async-done | bytes 1572880 | tf_op jit(solution)/shard_map/psum | solution.py:85
  224.5 1.0 constant_dynamic-slice_fusion
  225.5 1.0 broadcast_in_dim.19
  (34 shorter events, 3.9 us)
Async XLA Ops:
  6.5 11.4 %copy-start = (bf16[1,1024,384]{2,1,0:T(8,128)(2,1)S(1)}, bf16[1,1024,384]{2,1,0:T(8,128)(2,1)}, u32[]{:S(2)}) copy-start(bf16[1,1024,384]{2,1,0:T(8,128)(2,1)} %param.8) | copy-start | bytes 2359300
  11.6 11.2 %all-to-all-start = ((s32[8,1,64]{2,1,0:T(1,128)}), s32[8,1,64]{2,1,0:T(1,128)S(1)}, u32[]{:S(2)}, u32[]{:S(2)}) async-start(s32[8,1,64]{2,1,0:T(1,128)} %sub.34), calls=%async_computation | async-start | bytes 8192 | tf_op jit(solution)/shard_map/all_to_all | solution.py:60
  17.9 2.9 %copy-start.3 = (bf16[1,1024,256]{2,1,0:T(8,128)(2,1)S(1)}, bf16[1,1024,256]{2,1,0:T(8,128)(2,1)}, u32[]{:S(2)}) copy-start(bf16[1,1024,256]{2,1,0:T(8,128)(2,1)} %param.11) | copy-start | bytes 1572868
  20.9 20.3 %copy-start.5 = (bf16[1024,384]{1,0:T(8,128)(2,1)}, bf16[1024,384]{1,0:T(8,128)(2,1)S(1)}, u32[]{:S(2)}) copy-start(bf16[1024,384]{1,0:T(8,128)(2,1)S(1)} %fusion.22) | copy-start | bytes 2359300
  22.8 16.5 %all-to-all-start.2 = ((bf16[8,64,384]{2,1,0:T(8,128)(2,1)}), bf16[8,64,384]{2,1,0:T(8,128)(2,1)S(1)}, u32[]{:S(2)}, u32[]{:S(2)}) async-start(bf16[8,64,384]{2,1,0:T(8,128)(2,1)} %bitcast.17), calls=%async_computation.2 | async-start | bytes 786432 | tf_op jit(solution)/shard_map/all_to_all | solution.py:59
  27.6 47.1 %all-gather.9.cloned.1.call-start = ((), (), s32[]{:S(2)}) async-start(), calls=%async_computation.5 | async-start | bytes 1769472 | tf_op jit(solution)/shard_map/all_gather | solution.py:69
  41.2 59.1 %all-gather.5.cloned.1.call-start = ((), (), s32[]{:S(2)}) async-start(), calls=%async_computation.3 | async-start | bytes 1769472 | tf_op jit(solution)/shard_map/all_gather | solution.py:69
  45.0 29.7 %copy-start.2 = (bf16[2,256,2048]{2,1,0:T(8,128)(2,1)S(1)}, bf16[2,256,2048]{2,1,0:T(8,128)(2,1)}, u32[]{:S(2)}) copy-start(bf16[2,256,2048]{2,1,0:T(8,128)(2,1)} %param.12) | copy-start | bytes 6291460
  74.2 54.4 %all-gather.11.cloned.1.call-start = ((), (), s32[]{:S(2)}) async-start(), calls=%async_computation.6 | async-start | bytes 1769472 | tf_op jit(solution)/shard_map/all_gather | solution.py:73
  77.4 25.7 %copy-start.1 = (f32[2]{0:T(128)S(1)}, f32[2]{0:T(128)}, u32[]{:S(2)}) copy-start(f32[2]{0:T(128)} %param.13) | copy-start | bytes 28
  77.4 79.0 %all-gather.7.cloned.1.call-start = ((), (), s32[]{:S(2)}) async-start(), calls=%async_computation.4 | async-start | bytes 1769472 | tf_op jit(solution)/shard_map/all_gather | solution.py:73
  103.0 27.8 %copy-start.4 = (bf16[1,1024,256]{2,1,0:T(8,128)(2,1)S(1)}, bf16[1,1024,256]{2,1,0:T(8,128)(2,1)}, u32[]{:S(2)}) copy-start(bf16[1,1024,256]{2,1,0:T(8,128)(2,1)} %param.11) | copy-start | bytes 1572868
  103.1 121.4 %all-reduce.2.cloned.1.call-start = ((), (), s32[]{:S(2)}) async-start(), calls=%async_computation.7 | async-start | bytes 3145728 | tf_op jit(solution)/shard_map/psum | solution.py:85
Sparse Core Ops, SparseCore 0:
  41.3 33.2 all-gather.8
  76.3 23.9 all-gather.4
  101.9 26.7 all-gather.10
  130.1 26.3 all-gather.6
  164.8 59.6 all-reduce.1
where the time goes:
time: 234 us; the launch traced here: 233 us
  waiting for transfers between devices  141 us (60%)
  matrix products  33.3 us (14%)
  blocking collectives  25 us (11%)
  between operations  15.2 us (6%)
  starting transfers between devices  11.3 us (5%)
  local copies, waits for them, and re-layouts  5.35 us (2%)
    psum x1, waiting for transfers between devices, on_device(): whole_sum = lax.psum(accumulated, 'shift')  59.8 us
    all_gather x2, waiting for transfers between devices, on_device(): piece = lax.all_gather(interface_sol, 'sub', axis=0, tiled=True)  47.4 us
    all_to_all x1, blocking collectives, on_device(): lax.all_to_all(send_rows, 'sub', split_axis=0, concat_axis=0, tiled=True)  25 us
    all_gather x2, waiting for transfers between devices, on_device(): lax.all_gather(reduced_own, 'sub', axis=0, tiled=True)  23.2 us
    all_to_all x1, waiting for transfers between devices, on_device(): lax.all_to_all(send_rows, 'sub', split_axis=0, concat_axis=0, tiled=True)  10.4 us
    dot_general x2, matrix products, on_device(): jnp.dot(inverse, correction, preferred_element_type=jnp.float32)  9.15 us
    dot_general x2, matrix products, on_device(): jnp.dot(inverse, rhs_local, preferred_element_type=jnp.float32)  6.61 us
    all_to_all x1, starting transfers between devices, on_device(): lax.all_to_all(send_ids, 'sub', split_axis=0, concat_axis=0, tiled=True)  6.38 us
  transfers between devices with their start and end apart: 7, of which 7 were waited for; matrix products, arithmetic and copies ran while one was open for 11% of the time, Pallas kernels for 0%

commit v1 on v0

v1 whole, which is shorter than its diff:
```python
import functools

import jax
import jax.numpy as jnp
from jax import lax
from jax.experimental import pallas as pl
from jax.experimental.pallas import tpu as pltpu
from jax.sharding import PartitionSpec as P

MESH = pl.DeviceIdType.MESH
F32 = jnp.float32
BF16 = jnp.bfloat16


def dot(a, b):
    return jnp.dot(a, b, preferred_element_type=F32)


def dot_nt(a, b):
    return lax.dot_general(a, b, (((1,), (1,)), ((), ())), preferred_element_type=F32)


def ones_where(mask):
    return jnp.where(mask, 1.0, 0.0).astype(BF16)


def slot_select(index_row, start, rows, slots):
    touched = index_row.shape[1]
    hit = ones_where(lax.broadcasted_iota(jnp.int32, (rows, touched), 0) + start == index_row)
    member = dot_nt(jnp.ones((16, touched), BF16), hit)
    before = ones_where(
        lax.broadcasted_iota(jnp.int32, (rows, rows), 0)
        < lax.broadcasted_iota(jnp.int32, (rows, rows), 1)
    )
    rank = dot(member.astype(BF16), before)[0:1]
    place = jnp.where(member[0:1] > 0.5, rank, -1.0)
    chosen = ones_where(
        lax.broadcasted_iota(jnp.int32, (slots, rows), 0) == place.astype(jnp.int32)
    )
    return chosen, hit


def kernel(
    owners,
    shares,
    width,
    rhs_hbm,
    iface_hbm,
    inverse_hbm,
    couple_hbm,
    schur_hbm,
    weight_ref,
    owner_ref,
    index_ref,
    out_ref,
    rhs,
    iface,
    inverse,
    couple,
    schur,
    couple_t,
    schur_rhs,
    schur_picked,
    chosen,
    back,
    couple_slots,
    eliminated,
    gathered,
    x_send,
    x_recv,
    total,
    own_total,
    d_send,
    d_recv,
    load_sem,
    g_send,
    g_recv,
    c_send,
    c_recv,
    s_send,
    s_recv,
):
    me = lax.axis_index("sub")
    mine = lax.axis_index("shift")
    core = lax.rem(me, 2)
    sibling = me + 1 - 2 * core
    chip = me // 2
    chips = owners // 2
    shifts, rows, interface = schur.shape
    interior = rhs.shape[0]
    touched = couple.shape[1]
    slots = chosen.shape[1]
    share = interior // shares
    chunks = rhs.shape[1] // width

    loads = [
        pltpu.make_async_copy(rhs_hbm.at[0], rhs, load_sem.at[0]),
        pltpu.make_async_copy(couple_hbm.at[0], couple, load_sem.at[1]),
        pltpu.make_async_copy(schur_hbm, schur, load_sem.at[2]),
        pltpu.make_async_copy(iface_hbm, iface, load_sem.at[3]),
    ]
    inverse_loads = [
        pltpu.make_async_copy(inverse_hbm.at[j, 0], inverse.at[j], load_sem.at[4 + j])
        for j in range(shifts)
    ]
    loads[0].start()
    for load in inverse_loads:
        load.start()
    for load in loads[1:]:
        load.start()

    barrier = pltpu.get_barrier_semaphore()
    for d in range(1, owners):
        pl.semaphore_signal(
            barrier, inc=1, device_id={"sub": lax.rem(me + d, owners)}, device_id_type=MESH
        )
    for d in range(1, shares):
        pl.semaphore_signal(
            barrier, inc=1, device_id={"shift": lax.rem(mine + d, shares)}, device_id_type=MESH
        )

    def columns(c):
        return slice(c * width, (c + 1) * width)

    def block(c, source, to, way):
        return pltpu.make_async_remote_copy(
            src_ref=gathered.at[c, source],
            dst_ref=gathered.at[c, source],
            send_sem=g_send.at[c, source, way],
            recv_sem=g_recv.at[c, source],
            device_id={"sub": to},
            device_id_type=MESH,
        )

    def right(c, source):
        return block(c, source, lax.rem(me + 2, owners), 0)

    def left(c, source):
        return block(c, source, lax.rem(me + owners - 2, owners), 1)

    def across(c, source):
        return block(c, source, sibling, 2)

    def own_copies(c, act):
        @pl.when(chip < chips - 1)
        def _():
            act(right(c, me))

        @pl.when(chip > 0)
        def _():
            act(left(c, me))

        act(across(c, me))

    def hop_copies(c, hop, act, first):
        @pl.when(chip - 1 - hop >= 0)
        def _():
            source = me - 2 * (hop + 1)
            if first:
                right(c, source).wait_recv()

            @pl.when(chip < chips - 1)
            def _():
                act(right(c, source))

            act(across(c, source))

        @pl.when(chip + 1 + hop < chips)
        def _():
            source = me + 2 * (hop + 1)
            if first:
                left(c, source).wait_recv()

            @pl.when(chip > 0)
            def _():
                act(left(c, source))

            act(across(c, source))

    def start(copy):
        copy.start()

    def wait_send(copy):
        copy.wait_send()

    def send_own(c):
        own_copies(c, start)

    def hop_on(c, hop):
        if hop < chips - 1:
            hop_copies(c, hop, start, True)

    def eliminate(c):
        for j in range(shifts):
            if c == 0:
                inverse_loads[j].wait()
            solved = dot(inverse[j], rhs[:, columns(c)]).astype(BF16)
            eliminated[c, j] = solved
        if c == 0:
            loads[1].wait()
            couple_t[...] = couple[...].T
        for j in range(shifts):
            gathered[c, me, j] = dot(couple_t[...], eliminated[c, j]).astype(BF16)

    def index_row(position):
        return index_ref[pl.ds(owner_ref[position], 1), :]

    def slots_to(position, carry):
        chosen[position] = slot_select(index_row(position), me * rows, rows, slots)[0]
        return carry

    def slots_from(owner, carry):
        picks, hit = slot_select(index_row(me), owner * rows, rows, slots)
        back[owner] = dot(picks, hit).astype(BF16)
        return carry

    def pick_schur(position, carry):
        hit = ones_where(
            lax.broadcasted_iota(jnp.int32, (interface, touched), 0) == index_row(position)
        )
        flat = schur[...].reshape(shifts * rows, interface)
        schur_picked[position] = dot(flat, hit).astype(BF16)
        return carry

    def x_copy(c, to, sender):
        return pltpu.make_async_remote_copy(
            src_ref=x_send.at[c, to],
            dst_ref=x_recv.at[c, sender],
            send_sem=c_send.at[c, to],
            recv_sem=c_recv.at[c, sender],
            device_id={"sub": to},
            device_id_type=MESH,
        )

    def solve_interface(c):
        for z in range(chips):
            across(c, 2 * z + 1 - core).wait_recv()
        for j in range(shifts):
            x = schur_rhs[j, :, columns(c)]
            for p in range(owners):
                x = x - dot(schur_picked[p, j * rows : (j + 1) * rows], gathered[c, p, j])
            picked = dot(chosen[...].reshape(owners * slots, rows), x.astype(BF16))
            x_send[c, :, j] = picked.astype(BF16).reshape(owners, slots, width)

        def send(d, carry):
            to = lax.rem(me + d, owners)
            x_copy(c, to, me).start()
            return carry

        lax.fori_loop(1, owners, send, 0)
        x_recv[c, me] = x_send[c, me]

    def d_copy(c, to, sender):
        return pltpu.make_async_remote_copy(
            src_ref=d_send.at[c, to],
            dst_ref=d_recv.at[c, sender],
            send_sem=s_send.at[c, to],
            recv_sem=s_recv.at[c, sender],
            device_id={"shift": to},
            device_id_type=MESH,
        )

    def solve_interior(c):
        def receive(d, carry):
            sender = lax.rem(me + d, owners)
            x_copy(c, sender, sender).wait_recv()
            return carry

        lax.fori_loop(1, owners, receive, 0)
        acc = None
        for j in range(shifts):
            flat = x_recv[c, :, j].reshape(owners * slots, width)
            correction = dot(couple_slots[...], flat).astype(BF16)
            solved = eliminated[c, j].astype(F32) - dot(inverse[j], correction)
            term = weight_ref[j] * solved
            acc = term if acc is None else acc + term
        acc = acc.reshape(shares, share, width)
        d_send[c] = acc.astype(BF16)
        for d in range(1, shares):
            d_copy(c, lax.rem(mine + d, shares), mine).start()
        total[...] = acc
        own_total[c] = total[mine]

    def finish(c):
        acc = own_total[c]
        for d in range(1, shares):
            sender = lax.rem(mine + d, shares)
            d_copy(c, sender, sender).wait_recv()
            acc = acc + d_recv[c, sender].astype(F32)
        out_ref[:, columns(c)] = acc

    loads[0].wait()
    eliminate(0)
    pl.semaphore_wait(barrier, owners + shares - 2)
    send_own(0)

    def prepare_slots():
        lax.fori_loop(0, owners, slots_to, 0)
        lax.fori_loop(0, owners, slots_from, 0)
        couple_slots[...] = dot_nt(
            couple[...], back[...].reshape(owners * slots, touched)
        ).astype(BF16)

    def prepare_rhs():
        loads[2].wait()
        loads[3].wait()
        for j in range(shifts):
            schur_rhs[j] = dot(schur[j], iface[...])

    def prepare_schur(low, high):
        lax.fori_loop(low, high, pick_schur, 0)

    half = owners // 2
    work = [
        lambda: prepare_schur(0, half),
        lambda: prepare_schur(half, owners),
        prepare_slots,
    ]
    if chunks > 1:
        eliminate(1)
    prepare_rhs()
    steps = chunks + chips - 2
    for step in range(steps):
        for c in range(chunks):
            hop = step - c
            if 0 <= hop < chips - 1:
                hop_on(c, hop)
        complete = step - (chips - 2)
        if 0 <= complete < chunks:
            while work:
                work.pop(0)()
            solve_interface(complete)
        if step + 1 < chunks:
            send_own(step + 1)
        if step + 2 < chunks:
            eliminate(step + 2)
        if work:
            work.pop(0)()
    for c in range(chunks):
        solve_interior(c)
    for c in range(chunks):
        finish(c)

    for c in range(chunks):
        own_copies(c, wait_send)
        for hop in range(chips - 1):
            hop_copies(c, hop, wait_send, False)

        def sent(d, carry):
            to = lax.rem(me + d, owners)
            x_copy(c, to, me).wait_send()
            return carry

        lax.fori_loop(1, owners, sent, 0)
        for d in range(1, shares):
            d_copy(c, lax.rem(mine + d, shares), mine).wait_send()


def on_device(
    owners,
    shares,
    interior_rhs,
    interface_rhs,
    interior_inverse,
    coupling,
    schur_inverse,
    weights,
    owner_sub,
    index_blocks,
):
    _, interior, columns = interior_rhs.shape
    shifts, rows, interface = schur_inverse.shape
    touched = coupling.shape[2]
    slots = max(2, 2 * touched // owners)
    share = interior // shares
    width = 128
    chunks = columns // width
    whole = pl.BlockSpec(memory_space=pl.ANY)
    scalars = pl.BlockSpec(memory_space=pltpu.SMEM)
    vector = pl.BlockSpec(memory_space=pltpu.VMEM)
    result = pl.pallas_call(
        functools.partial(kernel, owners, shares, width),
        out_shape=jax.ShapeDtypeStruct((share, columns), F32),
        in_specs=[whole] * 5 + [scalars] * 2 + [vector],
        out_specs=vector,
        scratch_shapes=[
            pltpu.VMEM((interior, columns), BF16),
            pltpu.VMEM((interface, columns), BF16),
            pltpu.VMEM((shifts, interior, interior), BF16),
            pltpu.VMEM((interior, touched), BF16),
            pltpu.VMEM((shifts, rows, interface), BF16),
            pltpu.VMEM((touched, interior), BF16),
            pltpu.VMEM((shifts, rows, columns), F32),
            pltpu.VMEM((owners, shifts * rows, touched), BF16),
            pltpu.VMEM((owners, slots, rows), BF16),
            pltpu.VMEM((owners, slots, touched), BF16),
            pltpu.VMEM((interior, owners * slots), BF16),
            pltpu.VMEM((chunks, shifts, interior, width), BF16),
            pltpu.VMEM((chunks, owners, shifts, touched, width), BF16),
            pltpu.VMEM((chunks, owners, shifts, slots, width), BF16),
            pltpu.VMEM((chunks, owners, shifts, slots, width), BF16),
            pltpu.VMEM((shares, share, width), F32),
            pltpu.VMEM((chunks, share, width), F32),
            pltpu.VMEM((chunks, shares, share, width), BF16),
            pltpu.VMEM((chunks, shares, share, width), BF16),
            pltpu.SemaphoreType.DMA((4 + shifts,)),
            pltpu.SemaphoreType.DMA((chunks, owners, 3)),
            pltpu.SemaphoreType.DMA((chunks, owners)),
            pltpu.SemaphoreType.DMA((chunks, owners)),
            pltpu.SemaphoreType.DMA((chunks, owners)),
            pltpu.SemaphoreType.DMA((chunks, shares)),
            pltpu.SemaphoreType.DMA((chunks, shares)),
        ],
        compiler_params=pltpu.CompilerParams(
            collective_id=0, has_side_effects=True, vmem_limit_bytes=48 * 1024 * 1024
        ),
    )(
        interior_rhs,
        interface_rhs,
        interior_inverse,
        coupling,
        schur_inverse,
        weights,
        owner_sub,
        index_blocks,
    )
    return result[:, None, :]


def solution(mesh):
    in_specs = (
        P("sub", None, None),
        P(),
        P("shift", "sub", None, None),
        P("sub", None, None),
        P("shift", "sub", None),
        P("shift"),
        P(),
        P(),
    )
    out_specs = P("shift", "sub", None)
    body = functools.partial(on_device, mesh.shape["sub"], mesh.shape["shift"])
    return jax.shard_map(
        body, mesh=mesh, in_specs=in_specs, out_specs=out_specs, check_vma=False
    )
```

time: 234 us -> 70.4 us (0.30)
  waiting for transfers between devices: 141 us -> 0 us
  Pallas kernels: 0 us -> 61.7 us
  matrix products: 33.3 us -> 0 us
  blocking collectives: 25 us -> 0 us
  between operations: 15.2 us -> 0.02 us
  starting transfers between devices: 11.3 us -> 0 us
  local copies, waits for them, and re-layouts: 5.35 us -> 8.33 us
    all_gather x4 -> x0, waiting for transfers between devices: 70.6 us -> none  [the longest x2 47.4 us: on_device(): piece = lax.all_gather(interface_sol, 'sub', axis=0, tiled=True)]
    pallas_call x0 -> x1, Pallas kernels: none -> 61.7 us  [on_device(): pl.pallas_call(functools.partial(kernel, owners, shares, width), out_shap...]
    psum x1 -> x0, waiting for transfers between devices: 59.8 us -> none  [on_device(): whole_sum = lax.psum(accumulated, 'shift')]
    dot_general x12 -> x0, matrix products: 33.3 us -> none  [the longest x2 9.15 us: on_device(): jnp.dot(inverse, correction, preferred_element_type=jnp.float32)]
    all_to_all x1 -> x0, blocking collectives: 25 us -> none  [on_device(): lax.all_to_all(send_rows, 'sub', split_axis=0, concat_axis=0, tiled=True)]
    all_to_all x2 -> x0, starting transfers between devices: 11.2 us -> none  [the longest x1 6.38 us: on_device(): lax.all_to_all(send_ids, 'sub', split_axis=0, concat_axis=0, tiled=True)]
    all_to_all x2 -> x0, waiting for transfers between devices: 10.7 us -> none  [the longest x1 10.4 us: on_device(): lax.all_to_all(send_rows, 'sub', split_axis=0, concat_axis=0, tiled=True)]
    unnamed x12 -> x14, local copies, waits for them, and re-layouts: 0.03 us -> 7.18 us
  transfers between devices with their start and end apart: 7 -> 0, of which waited for: 7 -> 0; matrix products, arithmetic and copies ran while one was open for 11% -> 0% of each run, Pallas kernels for 0% -> 0%
where the time goes in v1:
time: 70.4 us; the launch traced here: 70.1 us
  Pallas kernels  61.7 us (88%)
  local copies, waits for them, and re-layouts  8.33 us (12%)
    pallas_call x1, Pallas kernels, on_device(): pl.pallas_call(functools.partial(kernel, owners, shares, width), out_shap...  61.7 us
    unnamed x14, local copies, waits for them, and re-layouts  7.18 us

profile of v1, /device:TPU:1, one launch (start us, length us, event | category | flops | bytes accessed | tf_op | source)
XLA Modules:
  0.0 70.1 jit_solution(5328859727852400863)
XLA Ops:
  0.0 0.0 copy-start
  0.0 1.6 %copy-done = bf16[2,256,2048]{2,1,0:T(8,128)(2,1)S(1)} copy-done((bf16[2,256,2048]{2,1,0:T(8,128)(2,1)S(1)}, bf16[2,256,2048]{2,1,0:T(8,128)(2,1)}, u32[]{:S(2)}) %copy-start) | copy-done | bytes 2097176
  1.6 0.0 copy-start.1
  1.6 1.4 %copy-done.1 = bf16[2048,384]{1,0:T(8,128)(2,1)S(1)} copy-done((bf16[2048,384]{1,0:T(8,128)(2,1)S(1)}, bf16[2048,384]{1,0:T(8,128)(2,1)}, u32[]{:S(2)}) %copy-start.1) | copy-done | bytes 1572888
  3.0 0.0 copy-start.2
  3.0 1.1 %copy-done.2 = bf16[1,1024,384]{2,1,0:T(8,128)(2,1)S(1)} copy-done((bf16[1,1024,384]{2,1,0:T(8,128)(2,1)S(1)}, bf16[1,1024,384]{2,1,0:T(8,128)(2,1)}, u32[]{:S(2)}) %copy-start.2) | copy-done | bytes 786456
  4.1 0.0 copy-start.3
  4.1 1.0 %copy-done.3 = bf16[1,1024,256]{2,1,0:T(8,128)(2,1)S(1)} copy-done((bf16[1,1024,256]{2,1,0:T(8,128)(2,1)S(1)}, bf16[1,1024,256]{2,1,0:T(8,128)(2,1)}, u32[]{:S(2)}) %copy-start.3) | copy-done | bytes 524312
  5.2 0.0 copy-start.4
  5.2 0.7 copy-done.4
  5.9 0.0 copy-start.5
  5.9 0.7 copy-done.5
  6.5 0.0 copy-start.6
  6.5 0.7 copy-done.6
  7.2 61.7 %shard_map.82 = f32[256,384]{1,0:T(8,128)S(1)} custom-call(bf16[1,1024,384]{2,1,0:T(8,128)(2,1)S(1)} %copy-done.2, bf16[2048,384]{1,0:T(8,128)(2,1)S(1)} %copy-done.1, bf16[2,1,1024,1024]{3,2,1,0:T(8,128)(2,1)} %inverse_hbm.1, bf16[1,1024,256]{2,1,0:T(8,128)(2,1)S(1)} %copy-done.3, bf16[2,256,2048]{2,1,0:T(8,128)(2,1)S(1)} %copy-done, f32[2]{0:T(128)S(1)} %copy-done.5, ...), custom_call_target="tpu_custom_call" | custom-call | tf_op jit(solution)/shard_map/pallas_call | solution.py:381
  68.9 1.2 %copy.9 = f32[256,1,384]{2,1,0:T(1,128)} copy(f32[256,1,384]{2,0,1:T(8,128)S(1)} %bitcast.1) | data formatting | bytes 786432 | tf_op jit(solution)/shard_map/broadcast_in_dim | solution.py:427
Async XLA Ops:
  0.0 1.6 %copy-start = (bf16[2,256,2048]{2,1,0:T(8,128)(2,1)S(1)}, bf16[2,256,2048]{2,1,0:T(8,128)(2,1)}, u32[]{:S(2)}) copy-start(bf16[2,256,2048]{2,1,0:T(8,128)(2,1)} %schur_hbm.1) | copy-start | bytes 6291460
  1.6 1.4 %copy-start.1 = (bf16[2048,384]{1,0:T(8,128)(2,1)S(1)}, bf16[2048,384]{1,0:T(8,128)(2,1)}, u32[]{:S(2)}) copy-start(bf16[2048,384]{1,0:T(8,128)(2,1)} %iface_hbm.1) | copy-start | bytes 4718596
  3.0 1.1 %copy-start.2 = (bf16[1,1024,384]{2,1,0:T(8,128)(2,1)S(1)}, bf16[1,1024,384]{2,1,0:T(8,128)(2,1)}, u32[]{:S(2)}) copy-start(bf16[1,1024,384]{2,1,0:T(8,128)(2,1)} %rhs_hbm.1) | copy-start | bytes 2359300
  4.1 1.0 %copy-start.3 = (bf16[1,1024,256]{2,1,0:T(8,128)(2,1)S(1)}, bf16[1,1024,256]{2,1,0:T(8,128)(2,1)}, u32[]{:S(2)}) copy-start(bf16[1,1024,256]{2,1,0:T(8,128)(2,1)} %couple_hbm.1) | copy-start | bytes 1572868
  5.2 0.7 copy-start.4
  5.9 0.7 copy-start.5
  6.5 0.7 copy-start.6

commit v2 on v1

--- a/solution.py
+++ b/solution.py
@@ -295,8 +295,10 @@
     send_own(0)
 
     def prepare_slots():
-        lax.fori_loop(0, owners, slots_to, 0)
-        lax.fori_loop(0, owners, slots_from, 0)
+        lax.fori_loop(0, owners, slots_to, 0, unroll=4)
+
+    def prepare_back():
+        lax.fori_loop(0, owners, slots_from, 0, unroll=4)
         couple_slots[...] = dot_nt(
             couple[...], back[...].reshape(owners * slots, touched)
         ).astype(BF16)
@@ -312,9 +314,9 @@
 
     half = owners // 2
     work = [
+        prepare_slots,
         lambda: prepare_schur(0, half),
         lambda: prepare_schur(half, owners),
-        prepare_slots,
     ]
     if chunks > 1:
         eliminate(1)
@@ -336,6 +338,7 @@
             eliminate(step + 2)
         if work:
             work.pop(0)()
+    prepare_back()
     for c in range(chunks):
         solve_interior(c)
     for c in range(chunks):
@@ -375,7 +378,7 @@
     share = interior // shares
     width = 128
     chunks = columns // width
-    whole = pl.BlockSpec(memory_space=pl.ANY)
+    whole = pl.BlockSpec(memory_space=pltpu.HBM)
     scalars = pl.BlockSpec(memory_space=pltpu.SMEM)
     vector = pl.BlockSpec(memory_space=pltpu.VMEM)
     result = pl.pallas_call(
@@ -412,7 +415,7 @@
             pltpu.SemaphoreType.DMA((chunks, shares)),
         ],
         compiler_params=pltpu.CompilerParams(
-            collective_id=0, has_side_effects=True, vmem_limit_bytes=48 * 1024 * 1024
+            collective_id=0, has_side_effects=True, vmem_limit_bytes=56 * 1024 * 1024
         ),
     )(
         interior_rhs,

time: 70.4 us -> 68.3 us (0.970)
  local copies, waits for them, and re-layouts: 8.33 us -> 2.15 us
  Pallas kernels: 61.7 us -> 65.9 us
    unnamed x14 -> x0, local copies, waits for them, and re-layouts: 7.18 us -> none
    pallas_call x1, Pallas kernels: 61.7 us -> 65.9 us  [on_device(): pl.pallas_call(functools.partial(kernel, owners, shares, width), out_shap...]
    broadcast_in_dim x1, local copies, waits for them, and re-layouts: 1.15 us -> 2.15 us  [on_device(): return result[:, None, :]]
where the time goes in v2:
time: 68.3 us; the launch traced here: 68.1 us
  Pallas kernels  65.9 us (96%)
  local copies, waits for them, and re-layouts  2.15 us (3%)
    pallas_call x1, Pallas kernels, on_device(): pl.pallas_call(functools.partial(kernel, owners, shares, width), out_shap...  65.9 us
    broadcast_in_dim x1, local copies, waits for them, and re-layouts, on_device(): return result[:, None, :]  2.15 us

profile of v2, /device:TPU:1, one launch (start us, length us, event | category | flops | bytes accessed | tf_op | source)
XLA Modules:
  0.0 68.1 jit_solution(1396021035359158957)
XLA Ops:
  0.0 65.9 %shard_map.82 = f32[256,384]{1,0:T(8,128)} custom-call(bf16[1,1024,384]{2,1,0:T(8,128)(2,1)} %rhs_hbm.1, bf16[2048,384]{1,0:T(8,128)(2,1)} %iface_hbm.1, bf16[2,1,1024,1024]{3,2,1,0:T(8,128)(2,1)} %inverse_hbm.1, bf16[1,1024,256]{2,1,0:T(8,128)(2,1)} %couple_hbm.1, bf16[2,256,2048]{2,1,0:T(8,128)(2,1)} %schur_hbm.1, f32[2]{0:T(128)} %weight_ref.1, ...), custom_call_target="tpu_custom_call" | custom-call | tf_op jit(solution)/shard_map/pallas_call | solution.py:384
  65.9 2.1 %copy.9 = f32[256,1,384]{2,1,0:T(1,128)} copy(f32[256,1,384]{2,0,1:T(8,128)} %bitcast.1) | data formatting | bytes 786432 | tf_op jit(solution)/shard_map/broadcast_in_dim | solution.py:430
